TPU v7x, 32 devices: a whole 2x2x4 slice. The times are simulated.
32 devices in a mesh: rows: 16 (over z, y, core), rep: 2 (over x).
Axes of the slice: x: 2, y: 2, z: 4, core: 2. Of those that a mesh axis runs over, the one named last changes fastest.
Arguments:
- embeddings: bfloat16 [11264, 1024], P(('rows', 'rep')), may hold values from -6 to 6
- owner_ids: int32 [11264, 1], P(('rows', 'rep')), may hold values from 0 to 15; in each aligned block of 352 rows (0 to 351, 352 to 703, ...) at most 64 rows name the same one
- live_mask: int32 [11264], P(('rows', 'rep')), may hold values 0 or 1
Outputs:
- neighbour_means: bfloat16 [11264, 1024], P(('rows', 'rep'))
Inputs may be any that keep to these rules, and one draw needn't show every extreme that they name: `owner_ids`: among the rows of one device, at most 64 name the same owner, and in every draw some owner is named by exactly 64 of them.
All inputs are finite; a program needn't handle non-finite values. Where the computation divides by a largest or mean magnitude, that divisor is 1e-20 or more. No bound on the sum of `live_mask` on one device may be relied on, other than what follows from the above.
Results may differ from a plain program's by a relative error of at most 0.0017.
The roundings to bfloat16 on the way count: a program that leaves them out, or rounds other values in their place, can miss the bound.
Values may be sent and summed in bfloat16 or wider, within the bound.
A program may use at most 64 MiB of HBM per device.

v0:
```python
import jax
import jax.numpy as jnp
from jax import lax
from jax.sharding import PartitionSpec as P

BUCKET = 1024
JOIN_ROWS = 8192
KERNEL_SCALE = 4.0
EPSILON = 1e-06
SPLIT = lax.Precision.HIGH
PRECISE = lax.Precision.HIGHEST


def block_positions(owner_block, owners, slot_cap):
    rows = owner_block.shape[0]
    same = owner_block[:, None] == owner_block[None, :]
    index = jnp.arange(rows, dtype=jnp.int32)
    earlier = index[None, :] < index[:, None]
    slot_rank = jnp.sum((same & earlier).astype(jnp.int32), axis=1)
    return owner_block * slot_cap + slot_rank


def whiten(embedded, inverse_root):
    mapped = jnp.dot(embedded, inverse_root, preferred_element_type=jnp.float32)
    return (mapped * lax.rsqrt(jnp.mean(mapped * mapped, axis=1, keepdims=True) + EPSILON)).astype(
        jnp.bfloat16
    )


def root_of(moment):
    y = moment / jnp.max(jnp.sum(jnp.abs(moment), axis=1))
    eye = jnp.eye(y.shape[0], dtype=jnp.float32)
    square = jnp.dot(y, y, precision=SPLIT)
    inner = 1.6875 * eye - 0.5625 * y + 0.0625 * square
    return (2.25 * eye - 2.4375 * y + jnp.dot(square, inner, precision=SPLIT)).astype(jnp.bfloat16)


def masked_means(queries, members, same, alive):
    scores = lax.dot_general(
        queries, members, (((1,), (1,)), ((), ())), preferred_element_type=jnp.float32
    )
    weights = jnp.where(same, jnp.exp(KERNEL_SCALE * (scores / members.shape[1] - 1.0)), 0.0)
    denominator = jnp.sum(weights, axis=1, keepdims=True)
    summed = jnp.dot(weights.astype(jnp.bfloat16), members, preferred_element_type=jnp.float32)
    averaged = summed / jnp.where(alive[:, None] > 0, denominator, 1.0)
    normed = averaged * lax.rsqrt(jnp.mean(averaged * averaged, axis=1, keepdims=True) + EPSILON)
    return (normed * alive[:, None]).astype(jnp.bfloat16)


def spread(values, positions, slots_all):
    return jnp.zeros((slots_all,) + values.shape[1:], values.dtype).at[positions].set(values)


def by_exchange(embeddings, owner_ids, live_mask):
    rows_here, columns = embeddings.shape
    owners = lax.axis_size("rows")
    slot_cap = BUCKET // owners
    positions = block_positions(owner_ids[:, 0], owners, slot_cap)
    live_rows = live_mask.astype(jnp.bfloat16)
    masked = embeddings * live_rows[:, None]
    partial_moment = lax.dot_general(
        masked, masked, (((0,), (0,)), ((), ())), preferred_element_type=jnp.float32
    )
    inverse_root = root_of(lax.psum(partial_moment, ("rows", "rep")))
    whitened = whiten(embeddings, inverse_root)

    def swapped(values):
        return lax.all_to_all(values, "rows", split_axis=0, concat_axis=0, tiled=True)

    members = swapped(
        spread(whitened, positions, BUCKET).reshape(owners, slot_cap, columns)
    ).reshape(BUCKET, columns)
    alive = swapped(spread(live_rows, positions, BUCKET).reshape(owners, slot_cap))
    alive = alive.reshape(BUCKET).astype(jnp.float32)
    means = masked_means(members, members, alive[None, :] > 0, alive)
    returned = swapped(means.reshape(owners, slot_cap, columns))
    return returned.reshape(BUCKET, columns)[positions]


def by_gather(embeddings, owner_ids, live_mask):
    rows_here, columns = embeddings.shape
    owners = lax.axis_size("rows")
    key = jnp.where(live_mask > 0, owner_ids[:, 0], -1)
    keys = lax.all_gather(key, "rows", axis=0, tiled=True)
    everyone = lax.all_gather(embeddings, "rows", axis=0, tiled=True)
    share = columns // owners
    masked = everyone * (keys >= 0).astype(jnp.bfloat16)[:, None]
    own = lax.dynamic_slice_in_dim(masked, lax.axis_index("rows") * share, share, 1)
    part = lax.dot_general(
        own, masked, (((0,), (0,)), ((), ())), preferred_element_type=jnp.float32
    )
    part = lax.psum(part, "rep")
    moment = lax.all_gather(part, "rows", axis=0, tiled=True)
    whitened = whiten(everyone, root_of(moment))
    mine = lax.dynamic_slice_in_dim(whitened, lax.axis_index("rows") * rows_here, rows_here, 0)
    alive = (live_mask > 0).astype(jnp.float32)
    return masked_means(mine, whitened, owner_ids == keys[None, :], alive)


def solution(mesh):
    placed = (P(("rows", "rep"), None), P(("rows", "rep"), None), P(("rows", "rep")))

    def per_device(embeddings, owner_ids, live_mask):
        gathered = embeddings.shape[0] * mesh.shape["rows"]
        join = by_gather if gathered <= JOIN_ROWS else by_exchange
        return join(embeddings, owner_ids, live_mask)

    return jax.shard_map(
        per_device, mesh=mesh, in_specs=placed, out_specs=P(("rows", "rep"), None), check_vma=False
    )
```

profile of v0, /device:TPU:0, one launch (start us, length us, event | category | flops | bytes accessed | tf_op | source)
XLA Modules:
  0.0 265.8 jit_solution(3059865663002023440)
XLA Ops:
  6.5 0.0 all-gather.3.cloned.1.call-start
  6.5 0.7 all-gather.3.cloned.1.call-update
  7.3 0.0 all-reduce.3.cloned.1.call-start
  7.3 0.7 reduce.1
  8.0 1.2 dynamic-slice.4
  9.9 0.7 fusion.31
  10.6 0.1 select_dynamic-update-slice_fusion
  10.7 65.3 %all-reduce = s32[5632]{0:T(1024)S(1)} all-reduce(s32[5632]{0:T(1024)S(1)} %select_dynamic-update-slice_fusion), channel_id=1, replica_groups=mesh['rows'=16,'rep'=2] {'rows'}, use_global_device_ids=true, to_apply=%add | all-reduce | flops 5632 | bytes 45056
  76.0 31.2 %all-gather.3.cloned.1.call-done = bf16[5632,1024]{1,0:T(8,128)(2,1)} async-done(((bf16[352,1024]{1,0:T(8,128)(2,1)}), bf16[5632,1024]{1,0:T(8,128)(2,1)}) %all-gather.3.cloned.1.call-update) | async-done | bytes 11534352 | tf_op jit(solution)/shard_map/all_gather | solution.py:85
  107.2 7.0 %broadcast_multiply_fusion = bf16[5632,1024]{1,0:T(8,128)(2,1)S(1)} fusion(bf16[5632,1024]{1,0:T(8,128)(2,1)} %all-gather.3.cloned.1.call-done, bf16[5632]{0:T(1024)(128)(2,1)S(1)} %compare_convert_fusion), kind=kLoop, calls=%fused_computation.7 | loop fusion | flops 5767168 | bytes 23079936 | tf_op jit(solution)/shard_map/mul | solution.py:87
  114.2 3.3 %fusion.19 = f32[64,1024]{1,0:T(8,128)} fusion(bf16[5632,1024]{1,0:T(8,128)(2,1)S(1)} %broadcast_multiply_fusion, s32[]{:T(128)S(6)} %select_n.20), kind=kOutput, calls=%fused_computation.27 | convolution fusion | flops 738197504 | bytes 13238276 | tf_op jit(solution)/shard_map/dot_general | solution.py:89
  117.5 0.0 all-reduce.3.cloned.1.call-update
  117.5 0.0 all-gather.5.cloned.1.call-start
  117.6 21.7 %all-reduce.3.cloned.1.call-done = f32[64,1024]{1,0:T(8,128)} async-done(((f32[64,1024]{1,0:T(8,128)}), f32[64,1024]{1,0:T(8,128)}) %all-reduce.3.cloned.1.call-update) | async-done | bytes 262160 | tf_op jit(solution)/shard_map/psum | solution.py:92
  139.3 0.0 all-gather.5.cloned.1.call-update
  139.3 53.0 %all-gather.5.cloned.1.call-done = f32[1024,1024]{1,0:T(8,128)} async-done(((f32[64,1024]{1,0:T(8,128)}), f32[1024,1024]{1,0:T(8,128)}) %all-gather.5.cloned.1.call-update) | async-done | bytes 4194320 | tf_op jit(solution)/shard_map/all_gather | solution.py:93
  192.3 2.6 abs_reduce_fusion
  194.8 0.6 reduce_max.9
  195.4 0.0 copy-start
  195.4 11.7 %fusion.18 = f32[1024,1024]{1,0:T(8,128)S(1)} fusion(f32[1024,1024]{1,0:T(8,128)} %all-gather.5.cloned.1.call-done, f32[]{:T(128)} %reduce_max.9), kind=kOutput, calls=%fused_computation.24 | convolution fusion | flops 6443499520 | bytes 8388612 | tf_op jit(solution)/shard_map/dot_general | solution.py:33
  207.2 0.0 copy-done
  207.2 8.6 %add_convert_fusion = bf16[1024,1024]{1,0:T(8,128)(2,1)S(1)} fusion(f32[1024,1024]{1,0:T(8,128)S(1)} %fusion.18, f32[1024,1024]{1,0:T(8,128)S(1)} %copy-done, f32[]{:T(128)} %reduce_max.9), kind=kOutput, calls=%fused_computation.8 | convolution fusion | flops 6457131008 | bytes 10485764 | tf_op jit(solution)/shard_map/dot_general | solution.py:35
  215.8 19.5 %multiply_reduce_fusion = (f32[5632]{0:T(1024)S(1)}, f32[1024,5632]{1,0:T(8,128)}) fusion(bf16[1024,1024]{1,0:T(8,128)(2,1)S(1)} %add_convert_fusion, bf16[5632,1024]{1,0:T(8,128)(2,1)} %all-gather.3.cloned.1.call-done), kind=kOutput, calls=%fused_computation.1 | convolution fusion | flops 11822688256 | bytes 36722688 | tf_op jit(solution)/shard_map/dot_general | solution.py:24
  235.3 8.7 %multiply_convert_fusion = bf16[1024,5632]{1,0:T(8,128)(2,1)S(1)} fusion(f32[1024,5632]{1,0:T(8,128)} %get-tuple-element.8, f32[5632]{0:T(1024)S(1)} %add_rsqrt_fusion), kind=kLoop, calls=%fused_computation | loop fusion | flops 11534336 | bytes 34625536 | tf_op jit(solution)/shard_map/convert_element_type | solution.py:25
  244.0 7.7 %fusion.32 = (f32[352]{0:T(512)S(1)}, bf16[352,5632]{1,0:T(8,128)(2,1)}) fusion(bf16[1024,5632]{1,0:T(8,128)(2,1)S(1)} %multiply_convert_fusion, s32[]{:T(128)S(6)} %select_n.21, s32[5632]{0:T(1024)S(1)} %all-reduce, s32[352]{0:T(512)S(1)} %reduce.1), kind=kOutput, calls=%fused_computation.44 | convolution fusion | flops 4073963264 | bytes 16313732 | tf_op jit(solution)/shard_map/dot_general | solution.py:39
  251.7 6.5 %multiply_reduce_fusion.1 = (f32[352]{0:T(512)S(1)}, f32[352,1024]{1,0:T(8,128)S(1)}) fusion(f32[352]{0:T(512)S(1)} %compare_select_fusion, bf16[1024,5632]{1,0:T(8,128)(2,1)S(1)} %multiply_convert_fusion, bf16[352,5632]{1,0:T(8,128)(2,1)} %get-tuple-element.10), kind=kOutput, calls=%fused_computation.26 | convolution fusion | flops 4061167360 | bytes 16943872 | tf_op jit(solution)/shard_map/dot_general | solution.py:44
  258.2 1.1 multiply_convert_fusion.1
  (5 shorter events, 0.0 us)
Async XLA Ops:
  6.5 100.7 %all-gather.3.cloned.1.call-start = ((), (), s32[]{:S(2)}) async-start(), calls=%async_computation | async-start | bytes 12255232 | tf_op jit(solution)/shard_map/all_gather | solution.py:85
  7.3 132.0 %all-reduce.3.cloned.1.call-start = ((), (), s32[]{:S(2)}) async-start(), calls=%async_computation.1 | async-start | bytes 524288 | tf_op jit(solution)/shard_map/psum | solution.py:92
  117.5 74.8 %all-gather.5.cloned.1.call-start = ((), (), s32[]{:S(2)}) async-start(), calls=%async_computation.2 | async-start | bytes 4456448 | tf_op jit(solution)/shard_map/all_gather | solution.py:93
  195.4 11.7 %copy-start = (f32[1024,1024]{1,0:T(8,128)S(1)}, f32[1024,1024]{1,0:T(8,128)}, u32[]{:S(2)}) copy-start(f32[1024,1024]{1,0:T(8,128)} %all-gather.5.cloned.1.call-done) | copy-start | bytes 12582916
Sparse Core Ops, SparseCore 0:
  9.6 97.5 all-gather.2
  117.6 21.6 all-reduce.2
  141.7 50.5 all-gather.4
where the time goes:
time: 266 us
  waiting for transfers between devices  107 us (40%)
  blocking collectives  65.3 us (25%)
  matrix products  57.3 us (22%)
  other arithmetic  21.4 us (8%)
  between operations  13.8 us (5%)
    unnamed x1, blocking collectives  65.3 us
    all_gather x1, waiting for transfers between devices, by_gather(): moment = lax.all_gather(part, 'rows', axis=0, tiled=True)  53 us
    all_gather x1, waiting for transfers between devices, by_gather(): everyone = lax.all_gather(embeddings, 'rows', axis=0, tiled=True)  31.2 us
    psum x1, waiting for transfers between devices, by_gather(): part = lax.psum(part, 'rep')  21.7 us
    dot_general x1, matrix products, whiten(): mapped = jnp.dot(embedded, inverse_root, preferred_element_type=jnp.float32)  19.5 us
    dot_general x1, matrix products, root_of(): square = jnp.dot(y, y, precision=SPLIT)  11.7 us
    convert_element_type x1, other arithmetic, whiten(): (mapped * lax.rsqrt(jnp.mean(mapped * mapped, axis=1, keepdims=True) + EP...  8.69 us
    dot_general x1, matrix products, root_of(): jnp.dot(square, inner, precision=SPLIT)  8.6 us
  transfers between devices with their start and end apart: 3, of which 3 were waited for; matrix products, arithmetic and copies ran while one was open for 1% of the time, Pallas kernels for 0%

commit v1 on v0

--- a/solution.py
+++ b/solution.py
@@ -89,7 +89,8 @@
     part = lax.dot_general(
         own, masked, (((0,), (0,)), ((), ())), preferred_element_type=jnp.float32
     )
-    part = lax.psum(part, "rep")
+    parts = lax.all_gather(part, "rep", axis=0, tiled=False)
+    part = parts.sum(axis=0)
     moment = lax.all_gather(part, "rows", axis=0, tiled=True)
     whitened = whiten(everyone, root_of(moment))
     mine = lax.dynamic_slice_in_dim(whitened, lax.axis_index("rows") * rows_here, rows_here, 0)

time: 266 us -> 250 us (0.940)
  waiting for transfers between devices: 107 us -> 81.1 us
  blocking collectives: 65.3 us -> 74.4 us
    psum x1 -> x0, waiting for transfers between devices: 21.7 us -> none  [by_gather(): part = lax.psum(part, 'rep')]
    all_gather x0 -> x1, blocking collectives: none -> 9.15 us  [by_gather(): parts = lax.all_gather(part, 'rep', axis=0, tiled=False)]
    all_gather x1, waiting for transfers between devices: 53 us -> 49.1 us  [by_gather(): moment = lax.all_gather(part, 'rows', axis=0, tiled=True)]
  transfers between devices with their start and end apart: 3 -> 2, of which waited for: 3 -> 2; matrix products, arithmetic and copies ran while one was open for 1% -> 1% of each run, Pallas kernels for 0% -> 0%
where the time goes in v1:
time: 250 us
  waiting for transfers between devices  81.1 us (32%)
  blocking collectives  74.4 us (30%)
  matrix products  56.6 us (23%)
  other arithmetic  22.1 us (9%)
  between operations  14.1 us (6%)
    unnamed x1, blocking collectives  65.3 us
    all_gather x1, waiting for transfers between devices, by_gather(): moment = lax.all_gather(part, 'rows', axis=0, tiled=True)  49.1 us
    all_gather x1, waiting for transfers between devices, by_gather(): everyone = lax.all_gather(embeddings, 'rows', axis=0, tiled=True)  31.2 us
    dot_general x1, matrix products, whiten(): mapped = jnp.dot(embedded, inverse_root, preferred_element_type=jnp.float32)  19.5 us
    dot_general x1, matrix products, root_of(): square = jnp.dot(y, y, precision=SPLIT)  11.7 us
    all_gather x1, blocking collectives, by_gather(): parts = lax.all_gather(part, 'rep', axis=0, tiled=False)  9.15 us
    convert_element_type x1, other arithmetic, whiten(): (mapped * lax.rsqrt(jnp.mean(mapped * mapped, axis=1, keepdims=True) + EP...  8.69 us
    dot_general x1, matrix products, root_of(): jnp.dot(square, inner, precision=SPLIT)  8.6 us
  transfers between devices with their start and end apart: 2, of which 2 were waited for; matrix products, arithmetic and copies ran while one was open for 1% of the time, Pallas kernels for 0%

profile of v1, /device:TPU:0, one launch (start us, length us, event | category | flops | bytes accessed | tf_op | source)
XLA Modules:
  0.0 249.6 jit_solution(2861297987380609151)
XLA Ops:
  6.5 0.0 all-gather.4.cloned.1.call-start
  6.5 0.7 all-gather.4.cloned.1.call-update
  7.3 0.0 all-gather.6.cloned.1.call-start
  7.3 0.7 reduce.1
  8.0 1.2 dynamic-slice.4
  9.9 0.7 fusion.31
  10.6 0.1 select_dynamic-update-slice_fusion
  10.7 65.3 %all-reduce = s32[5632]{0:T(1024)S(1)} all-reduce(s32[5632]{0:T(1024)S(1)} %select_dynamic-update-slice_fusion), channel_id=1, replica_groups=mesh['rows'=16,'rep'=2] {'rows'}, use_global_device_ids=true, to_apply=%add | all-reduce | flops 5632 | bytes 45056
  76.0 31.2 %all-gather.4.cloned.1.call-done = bf16[5632,1024]{1,0:T(8,128)(2,1)} async-done(((bf16[352,1024]{1,0:T(8,128)(2,1)}), bf16[5632,1024]{1,0:T(8,128)(2,1)}) %all-gather.4.cloned.1.call-update) | async-done | bytes 11534352 | tf_op jit(solution)/shard_map/all_gather | solution.py:85
  107.2 7.0 %broadcast_multiply_fusion = bf16[5632,1024]{1,0:T(8,128)(2,1)S(1)} fusion(bf16[5632,1024]{1,0:T(8,128)(2,1)} %all-gather.4.cloned.1.call-done, bf16[5632]{0:T(1024)(128)(2,1)S(1)} %compare_convert_fusion), kind=kLoop, calls=%fused_computation.7 | loop fusion | flops 5767168 | bytes 23079936 | tf_op jit(solution)/shard_map/mul | solution.py:87
  114.2 2.6 %fusion.19 = f32[64,1024]{1,0:T(8,128)S(1)} fusion(bf16[5632,1024]{1,0:T(8,128)(2,1)S(1)} %broadcast_multiply_fusion, s32[]{:T(128)S(6)} %select_n.20), kind=kOutput, calls=%fused_computation.27 | convolution fusion | flops 738197504 | bytes 13238276 | tf_op jit(solution)/shard_map/dot_general | solution.py:89
  116.8 9.1 %all-gather = f32[128,1024]{1,0:T(8,128)S(1)} all-gather(f32[64,1024]{1,0:T(8,128)S(1)} %fusion.19), channel_id=2, replica_groups=mesh['rows'=16,'rep'=2] {'rep'}, dimensions={0}, use_global_device_ids=true | all-gather | bytes 786432 | tf_op jit(solution)/shard_map/all_gather | solution.py:92
  125.9 0.7 reduce_sum.45
  126.7 0.0 all-gather.6.cloned.1.call-update
  126.7 49.1 %all-gather.6.cloned.1.call-done = f32[1024,1024]{1,0:T(8,128)} async-done(((f32[64,1024]{1,0:T(8,128)}), f32[1024,1024]{1,0:T(8,128)}) %all-gather.6.cloned.1.call-update) | async-done | bytes 4194320 | tf_op jit(solution)/shard_map/all_gather | solution.py:94
  175.8 2.6 %abs_reduce_fusion = f32[1024]{0:T(1024)S(1)} fusion(f32[1024,1024]{1,0:T(8,128)} %all-gather.6.cloned.1.call-done), kind=kLoop, calls=%fused_computation.15 | loop fusion | flops 2096128 | bytes 4198400 | tf_op jit(solution)/shard_map/reduce_sum | solution.py:31
  178.4 0.6 reduce_max.9
  179.0 0.0 copy-start
  179.0 11.7 %fusion.18 = f32[1024,1024]{1,0:T(8,128)S(1)} fusion(f32[1024,1024]{1,0:T(8,128)} %all-gather.6.cloned.1.call-done, f32[]{:T(128)} %reduce_max.9), kind=kOutput, calls=%fused_computation.24 | convolution fusion | flops 6443499520 | bytes 8388612 | tf_op jit(solution)/shard_map/dot_general | solution.py:33
  190.7 0.0 copy-done
  190.7 8.6 %add_convert_fusion = bf16[1024,1024]{1,0:T(8,128)(2,1)S(1)} fusion(f32[1024,1024]{1,0:T(8,128)S(1)} %fusion.18, f32[1024,1024]{1,0:T(8,128)S(1)} %copy-done, f32[]{:T(128)} %reduce_max.9), kind=kOutput, calls=%fused_computation.8 | convolution fusion | flops 6457131008 | bytes 10485764 | tf_op jit(solution)/shard_map/dot_general | solution.py:35
  199.3 19.5 %multiply_reduce_fusion = (f32[5632]{0:T(1024)S(1)}, f32[1024,5632]{1,0:T(8,128)}) fusion(bf16[1024,1024]{1,0:T(8,128)(2,1)S(1)} %add_convert_fusion, bf16[5632,1024]{1,0:T(8,128)(2,1)} %all-gather.4.cloned.1.call-done), kind=kOutput, calls=%fused_computation.1 | convolution fusion | flops 11822688256 | bytes 36722688 | tf_op jit(solution)/shard_map/dot_general | solution.py:24
  218.8 8.7 %multiply_convert_fusion = bf16[1024,5632]{1,0:T(8,128)(2,1)S(1)} fusion(f32[1024,5632]{1,0:T(8,128)} %get-tuple-element.8, f32[5632]{0:T(1024)S(1)} %add_rsqrt_fusion), kind=kLoop, calls=%fused_computation | loop fusion | flops 11534336 | bytes 34625536 | tf_op jit(solution)/shard_map/convert_element_type | solution.py:25
  227.5 7.7 %fusion.32 = (f32[352]{0:T(512)S(1)}, bf16[352,5632]{1,0:T(8,128)(2,1)}) fusion(bf16[1024,5632]{1,0:T(8,128)(2,1)S(1)} %multiply_convert_fusion, s32[]{:T(128)S(6)} %select_n.21, s32[5632]{0:T(1024)S(1)} %all-reduce, s32[352]{0:T(512)S(1)} %reduce.1), kind=kOutput, calls=%fused_computation.44 | convolution fusion | flops 4073963264 | bytes 16313732 | tf_op jit(solution)/shard_map/dot_general | solution.py:39
  235.2 6.5 %multiply_reduce_fusion.1 = (f32[352]{0:T(512)S(1)}, f32[352,1024]{1,0:T(8,128)S(1)}) fusion(f32[352]{0:T(512)S(1)} %compare_select_fusion, bf16[1024,5632]{1,0:T(8,128)(2,1)S(1)} %multiply_convert_fusion, bf16[352,5632]{1,0:T(8,128)(2,1)} %get-tuple-element.10), kind=kOutput, calls=%fused_computation.26 | convolution fusion | flops 4061167360 | bytes 16943872 | tf_op jit(solution)/shard_map/dot_general | solution.py:44
  241.7 1.1 multiply_convert_fusion.1
  (5 shorter events, 0.0 us)
Async XLA Ops:
  6.5 100.7 %all-gather.4.cloned.1.call-start = ((), (), s32[]{:S(2)}) async-start(), calls=%async_computation | async-start | bytes 12255232 | tf_op jit(solution)/shard_map/all_gather | solution.py:85
  7.3 168.6 %all-gather.6.cloned.1.call-start = ((), (), s32[]{:S(2)}) async-start(), calls=%async_computation.1 | async-start | bytes 4456448 | tf_op jit(solution)/shard_map/all_gather | solution.py:94
  179.0 11.7 %copy-start = (f32[1024,1024]{1,0:T(8,128)S(1)}, f32[1024,1024]{1,0:T(8,128)}, u32[]{:S(2)}) copy-start(f32[1024,1024]{1,0:T(8,128)} %all-gather.6.cloned.1.call-done) | copy-start | bytes 12582916
Sparse Core Ops, SparseCore 0:
  9.6 97.5 all-gather.3
  126.8 48.9 all-gather.5
